TPU v7x, 32 devices: a whole 2x2x4 slice. The times are simulated.
32 devices in a mesh: groups: 2 (over x), ctx: 16 (over z, y, core).
Axes of the slice: x: 2, y: 2, z: 4, core: 2. Of those that a mesh axis runs over, the one named last changes fastest.
Arguments:
- token_codes: int32 [4096, 3584], P(('groups', 'ctx')), parts along dimension 0, may hold values from 0 to 247, as said below
- scales: bfloat16 [4096], P(('groups', 'ctx')), parts along dimension 0, may hold values from 0.00390625 to 64
- routes: int32 [4096, 2], P(('groups', 'ctx')), parts along dimension 0, may hold values from 0 to 3, all different within a row; in each aligned block of 128 rows (0 to 127, 128 to 255, ...) at most 96 rows name the same one
- route_gates: float32 [4096, 2], P(('groups', 'ctx')), parts along dimension 0, may hold values from 0.1 to 1
- gate_proj: bfloat16 [16, 3584, 384], P('ctx'), may hold values from -0.09375 to 0.09375
- up_proj: bfloat16 [16, 3584, 384], P('ctx'), may hold values from -0.09375 to 0.09375
- down_proj: bfloat16 [16, 384, 3584], P('ctx'), may hold values from -0.15625 to 0.15625
Outputs:
- mixed: bfloat16 [4096, 3584], P(('groups', 'ctx')), parts along dimension 0
There are 2 independent parts, one for each index of `groups`. A program takes and returns all parts, laid end to end along the dimension named above; an argument that names none is the same for every part. Nothing has to cross between parts.
Inputs may be any that keep to these rules, and one draw needn't show every extreme that they name: In each aligned block of 128 tokens (the tokens of one device) no expert is named by more than 96 routes, a bound that some block reaches; the 2 experts of a token differ. `token_codes`: no code has exponent field 15.
All inputs are finite; a program needn't handle non-finite values.
Results may differ from a plain program's by a relative error of at most 0.0057.
Values may be sent and summed in bfloat16 or wider, within the bound.
A program may use at most 128 MiB of HBM per device.

v0:
```python
import jax
import jax.numpy as jnp
from jax import lax
from jax.sharding import PartitionSpec as P

SLICES = 4


def decode(token_codes):
    sign_bit = token_codes // 128
    exponent = token_codes // 8 % 16
    mantissa = (token_codes % 8).astype(jnp.float32)
    scaling = jnp.ones(token_codes.shape, jnp.float32)
    for bit_no in range(4):
        factor = jnp.float32(2.0**2**bit_no)
        scaling = scaling * jnp.where(exponent // 2**bit_no % 2 == 1, factor, jnp.float32(1.0))
    normal = (8.0 + mantissa) * scaling * jnp.float32(2.0 ** (-10))
    subnormal = mantissa * jnp.float32(2.0 ** (-9))
    magnitude = jnp.where(exponent == 0, subnormal, normal)
    return jnp.where(sign_bit == 1, -magnitude, magnitude).astype(jnp.bfloat16)


def local(token_codes, scales, routes, route_gates, gate_proj, up_proj, down_proj):
    tok_rows = token_codes.shape[0]
    features = token_codes.shape[1]
    top_k = routes.shape[1]
    devices = lax.axis_size("ctx")
    experts = devices // SLICES
    slot_count = 3 * tok_rows * top_k // (2 * experts)
    values = decode(token_codes)
    flat_ids = routes.reshape(-1)
    onehot = (flat_ids[:, None] == jnp.arange(experts, dtype=jnp.int32)[None, :]).astype(jnp.int32)
    before = jnp.cumsum(onehot, axis=0) - onehot
    slot_rank = jnp.sum(before * onehot, axis=1)
    target = (flat_ids * slot_count + slot_rank).reshape(tok_rows, top_k)
    places = jnp.arange(experts * slot_count, dtype=jnp.int32)
    chooser = jnp.sum(
        (target[None, :, :] == places[:, None, None]).astype(jnp.int32), axis=2
    ).astype(jnp.bfloat16)
    packed = jnp.dot(chooser, values, preferred_element_type=jnp.float32).astype(jnp.bfloat16)
    packed = packed.reshape(experts, slot_count, features)
    packed_scale = jnp.dot(chooser, scales[:, None], preferred_element_type=jnp.float32).astype(
        jnp.bfloat16
    )
    packed_scale = packed_scale.reshape(experts, slot_count)
    gate_block = gate_proj[0]
    up_block = up_proj[0]
    down_block = down_proj[0]
    outgoing = jnp.repeat(packed, SLICES, axis=0)
    outgoing_scale = jnp.repeat(packed_scale, SLICES, axis=0)
    slot_rows = lax.all_to_all(outgoing, "ctx", split_axis=0, concat_axis=0, tiled=True)
    lead_shape = slot_rows.shape[:-1]
    inputs = slot_rows.reshape(-1, features)
    row_scale = (
        lax.all_to_all(outgoing_scale, "ctx", split_axis=0, concat_axis=0, tiled=True)
        .reshape(-1, 1)
        .astype(jnp.float32)
    )
    gate_act = jnp.dot(inputs, gate_block, preferred_element_type=jnp.float32) * row_scale
    up_act = jnp.dot(inputs, up_block, preferred_element_type=jnp.float32) * row_scale
    hidden = (jax.nn.silu(gate_act) * up_act).astype(jnp.bfloat16)
    partial_value = jnp.dot(hidden, down_block, preferred_element_type=jnp.float32).astype(
        jnp.bfloat16
    )
    served = partial_value.reshape(lead_shape + (features,))
    returned = lax.all_to_all(served, "ctx", split_axis=0, concat_axis=0, tiled=True)
    summed = jnp.sum(
        returned.reshape(experts, SLICES, slot_count, features), axis=1, dtype=jnp.float32
    )
    summed = summed.reshape(experts * slot_count, features)
    picked = summed[target.reshape(-1)].reshape(tok_rows, top_k, features)
    return jnp.sum(route_gates[:, :, None] * picked, axis=1).astype(jnp.bfloat16)


def solution(mesh):
    placed = (
        P(("groups", "ctx"), None),
        P(("groups", "ctx")),
        P(("groups", "ctx"), None),
        P(("groups", "ctx"), None),
        P("ctx", None, None),
        P("ctx", None, None),
        P("ctx", None, None),
    )
    return jax.shard_map(
        local, mesh=mesh, in_specs=placed, out_specs=P(("groups", "ctx"), None), check_vma=False
    )
```

profile of v0, /device:TPU:15, one launch (start us, length us, event | category | flops | bytes accessed | tf_op | source)
XLA Modules:
  0.0 577.1 jit_solution(142630697096820638)
XLA Ops:
  0.0 0.0 copy-start
  0.0 0.9 copy.32
  0.9 0.1 eq.68
  1.1 0.1 eq.64
  1.2 1.2 reduce-window.6
  2.5 0.1 slice.10
  2.5 0.1 copy.35
  2.7 0.1 copy.36
  2.8 0.1 add_bitcast_fusion
  2.9 0.1 reduce_sum.41
  3.0 0.1 copy.37
  3.1 0.1 convert_reduce_fusion.1
  3.2 0.8 convolution_reduce_fusion
  4.0 0.1 reshape.101
  4.1 0.6 copy.38
  4.7 6.6 %all-to-all-start.1 = ((bf16[16,1,96]{2,1,0:T(2,128)(2,1)}), bf16[16,1,96]{2,1,0:T(2,128)(2,1)S(1)}, u32[]{:S(2)}, u32[]{:S(2)}) async-start(bf16[16,1,96]{2,1,0:T(2,128)(2,1)} %copy.38), calls=%async_computation.1 | async-start | bytes 16384 | tf_op jit(solution)/shard_map/all_to_all | solution.py:55
  11.3 12.0 %convolution_convert_fusion.1 = bf16[384,3584]{1,0:T(8,128)(2,1)} fusion(s32[128,3584]{1,0:T(8,128)} %param.7, s32[384,128]{1,0:T(8,128)S(1)} %convert_reduce_fusion.1), kind=kOutput, calls=%fused_computation.3 | convolution fusion | flops 415219712 | bytes 4784128 | tf_op jit(solution)/shard_map/dot_general | solution.py:40
  23.2 0.0 all-to-all-done.1
  23.2 6.9 %broadcast_in_dim.36 = bf16[4,4,96,3584]{3,2,1,0:T(8,128)(2,1)} broadcast(bf16[4,96,3584]{2,1,0:T(8,128)(2,1)} %bitcast.48), dimensions={0,2,3} | broadcast | bytes 13762560 | tf_op jit(solution)/shard_map/broadcast_in_dim | solution.py:49
  30.1 6.0 %all-to-all-start = ((bf16[16,96,3584]{2,1,0:T(8,128)(2,1)}), bf16[16,96,3584]{2,1,0:T(8,128)(2,1)}, u32[]{:S(2)}, u32[]{:S(2)}) async-start(bf16[16,96,3584]{2,1,0:T(8,128)(2,1)} %bitcast.46), calls=%async_computation | async-start | bytes 22020096 | tf_op jit(solution)/shard_map/all_to_all | solution.py:51
  36.1 0.1 reshape.105
  36.2 238.4 %all-to-all-done = bf16[16,96,3584]{2,1,0:T(8,128)(2,1)} async-done(((bf16[16,96,3584]{2,1,0:T(8,128)(2,1)}), bf16[16,96,3584]{2,1,0:T(8,128)(2,1)}, u32[]{:S(2)}, u32[]{:S(2)}) %all-to-all-start) | async-done | bytes 11010080 | tf_op jit(solution)/shard_map/all_to_all | solution.py:51
  274.6 10.6 %convolution_multiply_fusion.1 = f32[1536,384]{1,0:T(8,128)} fusion(bf16[1536,3584]{1,0:T(8,128)(2,1)} %bitcast.4, bf16[1,3584,384]{2,1,0:T(8,128)(2,1)} %param.11, f32[1536]{0:T(1024)S(1)} %reshape.105), kind=kOutput, calls=%fused_computation.7 | convolution fusion | flops 4228448256 | bytes 16128000 | tf_op jit(solution)/shard_map/dot_general | solution.py:59
  285.2 0.0 copy-done
  285.2 17.9 %convolution_convert_fusion = bf16[1536,3584]{1,0:T(8,128)(2,1)} fusion(bf16[1536,3584]{1,0:T(8,128)(2,1)} %bitcast.4, bf16[1,384,3584]{2,1,0:T(8,128)(2,1)S(1)} %copy-done, bf16[1,3584,384]{2,1,0:T(8,128)(2,1)} %param.12, f32[1536,384]{1,0:T(8,128)} %convolution_multiply_fusion.1, f32[1536]{0:T(1024)S(1)} %reshape.105), kind=kOutput, calls=%fused_computation.2 | convolution fusion | flops 8465350656 | bytes 29890560 | tf_op jit(solution)/shard_map/dot_general | solution.py:62
  303.1 0.0 copy-start.2
  303.1 5.1 all-to-all-start.2
  308.2 0.1 mul.91
  308.4 0.0 copy-done.2
  308.4 0.1 copy.31
  308.5 238.2 %all-to-all-done.2 = bf16[16,96,3584]{2,1,0:T(8,128)(2,1)} async-done(((bf16[16,96,3584]{2,1,0:T(8,128)(2,1)}), bf16[16,96,3584]{2,1,0:T(8,128)(2,1)}, u32[]{:S(2)}, u32[]{:S(2)}) %all-to-all-start.2) | async-done | bytes 11010080 | tf_op jit(solution)/shard_map/all_to_all | solution.py:66
  546.7 8.8 %convert_reduce_fusion = f32[4,96,3584]{2,1,0:T(8,128)} fusion(bf16[16,96,3584]{2,1,0:T(8,128)(2,1)} %all-to-all-done.2), kind=kLoop, calls=%fused_computation.1 | loop fusion | flops 9633792 | bytes 16515072 | tf_op jit(solution)/shard_map/reduce_sum | solution.py:67
  555.5 7.7 %gather_fusion = f32[256,3584]{1,0:T(8,128)} fusion(f32[384,3584]{1,0:T(8,128)} %bitcast.45, s32[1024]{0:T(1024)S(1)} %pad_clamp_fusion), kind=kCustom, calls=%fused_computation | custom fusion | bytes 7341056 | tf_op jit(solution)/shard_map/gather | solution.py:71
  563.2 0.0 copy-start.1
  563.2 5.7 reshape.104
  568.9 8.2 %multiply_reduce_fusion = bf16[128,3584]{1,0:T(8,128)(2,1)} fusion(f32[128,2,3584]{2,1,0:T(2,128)} %reshape.104, f32[128,2]{1,0:T(8,128)S(1)} %copy.31), kind=kLoop, calls=%fused_computation.4 | loop fusion | flops 1376256 | bytes 4588544 | tf_op jit(solution)/shard_map/reduce_sum | solution.py:72
  577.1 0.0 copy-done.1
  (9 shorter events, 0.1 us)
Async XLA Ops:
  0.0 285.2 %copy-start = (bf16[1,384,3584]{2,1,0:T(8,128)(2,1)S(1)}, bf16[1,384,3584]{2,1,0:T(8,128)(2,1)}, u32[]{:S(2)}) copy-start(bf16[1,384,3584]{2,1,0:T(8,128)(2,1)} %param.13) | copy-start | bytes 8257540
  4.7 18.5 %all-to-all-start.1 = ((bf16[16,1,96]{2,1,0:T(2,128)(2,1)}), bf16[16,1,96]{2,1,0:T(2,128)(2,1)S(1)}, u32[]{:S(2)}, u32[]{:S(2)}) async-start(bf16[16,1,96]{2,1,0:T(2,128)(2,1)} %copy.38), calls=%async_computation.1 | async-start | bytes 16384 | tf_op jit(solution)/shard_map/all_to_all | solution.py:55
  30.1 244.5 %all-to-all-start = ((bf16[16,96,3584]{2,1,0:T(8,128)(2,1)}), bf16[16,96,3584]{2,1,0:T(8,128)(2,1)}, u32[]{:S(2)}, u32[]{:S(2)}) async-start(bf16[16,96,3584]{2,1,0:T(8,128)(2,1)} %bitcast.46), calls=%async_computation | async-start | bytes 22020096 | tf_op jit(solution)/shard_map/all_to_all | solution.py:51
  303.1 5.2 copy-start.2
  303.1 243.6 %all-to-all-start.2 = ((bf16[16,96,3584]{2,1,0:T(8,128)(2,1)}), bf16[16,96,3584]{2,1,0:T(8,128)(2,1)}, u32[]{:S(2)}, u32[]{:S(2)}) async-start(bf16[16,96,3584]{2,1,0:T(8,128)(2,1)} %bitcast.47), calls=%async_computation.2 | async-start | bytes 22020096 | tf_op jit(solution)/shard_map/all_to_all | solution.py:66
  563.2 13.9 %copy-start.1 = (bf16[1,384,3584]{2,1,0:T(8,128)(2,1)S(1)}, bf16[1,384,3584]{2,1,0:T(8,128)(2,1)}, u32[]{:S(2)}) copy-start(bf16[1,384,3584]{2,1,0:T(8,128)(2,1)} %param.13) | copy-start | bytes 8257540
where the time goes:
time: 578 us; the launch traced here: 577 us
  waiting for transfers between devices  477 us (83%)
  matrix products  41.2 us (7%)
  local copies, waits for them, and re-layouts  23 us (4%)
  other arithmetic  18.5 us (3%)
  starting transfers between devices  17.7 us (3%)
    all_to_all x1, waiting for transfers between devices, local(): lax.all_to_all(outgoing, 'ctx', split_axis=0, concat_axis=0, tiled=True)  238 us
    all_to_all x1, waiting for transfers between devices, local(): lax.all_to_all(served, 'ctx', split_axis=0, concat_axis=0, tiled=True)  238 us
    dot_general x1, matrix products, local(): jnp.dot(hidden, down_block, preferred_element_type=jnp.float32)  17.9 us
    dot_general x1, matrix products, local(): jnp.dot(chooser, values, preferred_element_type=jnp.float32)  12 us
  transfers between devices with their start and end apart: 3, of which 2 were waited for; matrix products, arithmetic and copies ran while one was open for 2% of the time, Pallas kernels for 0%

commit v1 on v0

v1 whole, which is shorter than its diff:
```python
import functools

import jax
import jax.numpy as jnp
from jax import lax
from jax.experimental import pallas as pl
from jax.experimental.pallas import tpu as pltpu
from jax.sharding import PartitionSpec as P

SLICES = 4
LANES = 128
BF16 = jnp.bfloat16
F32 = jnp.float32


def decode(codes):
    exponent = (codes >> 3) & 15
    mantissa = codes & 7
    whole = jnp.where(exponent > 0, (mantissa + 8) << exponent, mantissa << 1)
    whole = jnp.where(codes >= 128, -whole, whole)
    return (whole.astype(F32) * F32(2.0**-10)).astype(BF16)


def kernel(
    experts, slot, tile,
    codes, scales, routes, gates, gate_hbm, up_hbm, down_hbm,
    out,
    w_gu, w_down, pack, recv, gu, hid, part, krecv, ysend, yrecv, hsend, hrecv,
    w_sem, z_s, z_r, y_s, y_r, c_s, c_r, l_s, l_r, k_s, k_r, q_s, q_r, h_s, h_r,
):
    tok, width = codes.shape
    ff = down_hbm.shape[1]
    quarter = SLICES * slot
    total = experts * slot
    group = lax.axis_index("groups")
    me = lax.axis_index("ctx")
    z, row, core = me // 4, (me // 2) % 2, me % 2

    def device(zz, yy, cc):
        return (group, zz * 4 + yy * 2 + cc)

    def ahead(step):
        return (z + step) % experts

    def behind(step):
        return (z + experts - step) % experts

    def remote(src, dst, send, arrive, to):
        return pltpu.make_async_remote_copy(
            src_ref=src, dst_ref=dst, send_sem=send, recv_sem=arrive,
            device_id=to, device_id_type=pl.DeviceIdType.MESH,
        )

    other_core = device(z, row, 1 - core)
    other_row = device(z, 1 - row, core)

    barrier = pltpu.get_barrier_semaphore()
    pl.semaphore_signal(barrier, inc=1, device_id=other_core, device_id_type=pl.DeviceIdType.MESH)
    pl.semaphore_signal(barrier, inc=1, device_id=other_row, device_id_type=pl.DeviceIdType.MESH)
    for step in range(1, experts):
        pl.semaphore_signal(
            barrier, inc=1, device_id=device(ahead(step), row, core),
            device_id_type=pl.DeviceIdType.MESH,
        )

    loads = [
        pltpu.make_async_copy(gate_hbm.at[0], w_gu.at[:, pl.ds(0, ff)], w_sem.at[0]),
        pltpu.make_async_copy(up_hbm.at[0], w_gu.at[:, pl.ds(ff, ff)], w_sem.at[1]),
        pltpu.make_async_copy(down_hbm.at[0], w_down, w_sem.at[2]),
    ]
    for load in loads:
        load.start()

    lane = lax.broadcasted_iota(jnp.int32, (tok, LANES), 1)
    named = []
    for k in range(2):
        rel = routes[:, k : k + 1] - z
        rel = jnp.where(rel < 0, rel + experts, rel)
        named.append(rel)
    hits = [(lane == rel).astype(F32) for rel in named]
    lower = (
        lax.broadcasted_iota(jnp.int32, (tok, tok), 0)
        > lax.broadcasted_iota(jnp.int32, (tok, tok), 1)
    ).astype(F32).astype(BF16)
    ranks = jnp.dot(lower, (hits[0] + hits[1]).astype(BF16), preferred_element_type=F32)
    places = lax.broadcasted_iota(jnp.int32, (tok, total), 1).astype(F32)
    chosen = []
    for k in range(2):
        rank = jnp.sum(ranks * hits[k], axis=1, keepdims=True)
        place = named[k].astype(F32) * F32(slot) + rank
        chosen.append((places == place).astype(F32))
    chooser = (chosen[0] + chosen[1]).T.astype(BF16)
    mixing = gates[:, 0:1] * chosen[0] + gates[:, 1:2] * chosen[1]
    mix_hi = mixing.astype(BF16)
    mix_lo = (mixing - mix_hi.astype(F32)).astype(BF16)

    own = pl.multiple_of((row * 2 + core) * slot, 16)
    packed_scale = jnp.dot(chooser, scales[...], preferred_element_type=F32).astype(BF16)
    recv[pl.ds(own, slot), pl.ds(width, LANES)] = packed_scale[:slot]
    pack[:, pl.ds(width, LANES)] = packed_scale[slot:]

    @pl.loop(0, width // tile)
    def _(n):
        cols = pl.ds(pl.multiple_of(n * tile, tile), tile)
        rows = jnp.dot(chooser, decode(codes[:, cols]), preferred_element_type=F32).astype(BF16)
        recv[pl.ds(own, slot), cols] = rows[:slot]
        pack[:, cols] = rows[slot:]

    pl.semaphore_wait(barrier, experts + 1)

    def packet(step, yy, cc):
        return recv.at[pl.ds(pl.multiple_of(step * quarter + (yy * 2 + cc) * slot, 16), slot)]

    def slab(ref, step):
        return ref.at[pl.ds(pl.multiple_of(step * slot, 16), slot)]

    def send_z(step):
        return remote(
            slab(pack, step - 1), packet(step, row, core), z_s.at[step], z_r.at[step],
            device(ahead(step), row, core),
        )

    def send_y(step):
        src = packet(step, row, core)
        return remote(src, src, y_s.at[step], y_r.at[step], other_row)

    def send_c(step):
        src = packet(step, row, core)
        return remote(src, src, c_s.at[step], c_r.at[step], other_core)

    def send_l(step):
        src = packet(step, 1 - row, core)
        return remote(src, src, l_s.at[step], l_r.at[step], other_core)

    def part_rows(step, yy, cc):
        start = (step % 2) * quarter + (yy * 2 + cc) * slot
        return pl.ds(pl.multiple_of(start, 16), slot)

    def kept(step, yy):
        return pl.ds(pl.multiple_of((step * 2 + yy) * slot, 16), slot)

    def send_k(step, yy):
        return remote(
            part.at[part_rows(step, yy, 1 - core)], krecv.at[kept(step, yy)],
            k_s.at[step * 2 + yy], k_r.at[step * 2 + yy], other_core,
        )

    def send_q(step):
        return remote(
            slab(ysend, step % 2), slab(yrecv, step), q_s.at[step], q_r.at[step], other_row
        )

    def send_h(step):
        return remote(
            slab(hsend, step), slab(hrecv, step), h_s.at[step], h_r.at[step],
            device(behind(step), row, core),
        )

    for step in range(1, experts):
        send_z(step).start()
    send_y(0).start()
    send_c(0).start()
    for load in loads:
        load.wait()

    def finish(step):
        send_k(step, row).wait_recv()
        send_q(step).wait_recv()

        @pl.loop(0, width // tile)
        def _(n):
            cols = pl.ds(pl.multiple_of(n * tile, tile), tile)
            value = (
                part[part_rows(step, row, core), cols].astype(F32)
                + krecv[kept(step, row), cols].astype(F32)
                + slab(yrecv, step)[:, cols].astype(F32)
            ).astype(BF16)

            @pl.when(step > 0)
            def _():
                hsend[pl.ds(pl.multiple_of(step * slot, 16), slot), cols] = value

            @pl.when(step == 0)
            def _():
                hrecv[pl.ds(0, slot), cols] = value

        @pl.when(step > 0)
        def _():
            send_h(step).start()

        send_k(step, 0).wait_send()
        send_k(step, 1).wait_send()

    def one_group(step, carry):
        @pl.when(step + 1 < experts)
        def _():
            send_z(step + 1).wait_recv()
            send_y(step + 1).start()
            send_c(step + 1).start()

        send_y(step).wait_recv()
        send_l(step).start()
        send_c(step).wait_recv()
        send_l(step).wait_recv()

        rows = pl.ds(pl.multiple_of(step * quarter, 16), quarter)

        @pl.loop(0, 2 * ff // 256)
        def _(n):
            cols = pl.ds(pl.multiple_of(n * 256, 256), 256)
            gu[:, cols] = jnp.dot(
                recv[rows, pl.ds(0, width)], w_gu[:, cols], preferred_element_type=F32
            )

        @pl.loop(0, SLICES)
        def _(n):
            some = pl.ds(pl.multiple_of(n * slot, 16), slot)
            where = pl.ds(pl.multiple_of(step * quarter + n * slot, 16), slot)
            scale = recv[where, pl.ds(width, LANES)].astype(F32)[:, :1]
            a = gu[some, pl.ds(0, ff)] * scale
            b = gu[some, pl.ds(ff, ff)] * scale
            hid[some, :] = (a / (1.0 + jnp.exp(-a)) * b).astype(BF16)

        base = pl.ds(pl.multiple_of((step % 2) * quarter, 16), quarter)

        @pl.loop(0, width // tile)
        def _(n):
            cols = pl.ds(pl.multiple_of(n * tile, tile), tile)
            part[base, cols] = jnp.dot(
                hid[...], w_down[:, cols], preferred_element_type=F32
            ).astype(BF16)

        send_k(step, 1 - row).start()
        send_k(step, row).start()

        @pl.when(step >= 2)
        def _():
            send_q(step - 2).wait_send()

        send_k(step, 1 - row).wait_recv()

        @pl.loop(0, width // tile)
        def _(n):
            cols = pl.ds(pl.multiple_of(n * tile, tile), tile)
            ysend[pl.ds(pl.multiple_of((step % 2) * slot, 16), slot), cols] = (
                part[part_rows(step, 1 - row, core), cols].astype(F32)
                + krecv[kept(step, 1 - row), cols].astype(F32)
            ).astype(BF16)

        send_q(step).start()

        @pl.when(step > 0)
        def _():
            finish(step - 1)

        return carry

    lax.fori_loop(0, experts, one_group, 0)
    finish(experts - 1)

    for step in range(1, experts):
        send_h(step).wait_recv()

    @pl.loop(0, width // tile)
    def _(n):
        cols = pl.ds(pl.multiple_of(n * tile, tile), tile)
        rows = hrecv[:, cols]
        out[:, cols] = (
            jnp.dot(mix_hi, rows, preferred_element_type=F32)
            + jnp.dot(mix_lo, rows, preferred_element_type=F32)
        ).astype(BF16)

    for step in range(experts):
        send_y(step).wait_send()
        send_c(step).wait_send()
        send_l(step).wait_send()
        if step >= experts - 2:
            send_q(step).wait_send()
        if step > 0:
            send_z(step).wait_send()
            send_h(step).wait_send()


def local(token_codes, scales, routes, route_gates, gate_proj, up_proj, down_proj):
    tok, width = token_codes.shape
    ff = gate_proj.shape[2]
    experts = lax.axis_size("ctx") // SLICES
    cap = 3 * tok * routes.shape[1] // (2 * experts)
    slot = -(-cap // 16) * 16
    total = experts * slot
    vmem = pl.BlockSpec(memory_space=pltpu.VMEM)
    hbm = pl.BlockSpec(memory_space=pl.ANY)
    dma = pltpu.SemaphoreType.DMA
    return pl.pallas_call(
        functools.partial(kernel, experts, slot, 512),
        out_shape=jax.ShapeDtypeStruct((tok, width), BF16),
        in_specs=[vmem] * 4 + [hbm] * 3,
        out_specs=vmem,
        scratch_shapes=[
            pltpu.VMEM((width, 2 * ff), BF16),
            pltpu.VMEM((ff, width), BF16),
            pltpu.VMEM((total - slot, width + LANES), BF16),
            pltpu.VMEM((SLICES * total, width + LANES), BF16),
            pltpu.VMEM((SLICES * slot, 2 * ff), F32),
            pltpu.VMEM((SLICES * slot, ff), BF16),
            pltpu.VMEM((2 * SLICES * slot, width), BF16),
            pltpu.VMEM((2 * total, width), BF16),
            pltpu.VMEM((2 * slot, width), BF16),
            pltpu.VMEM((total, width), BF16),
            pltpu.VMEM((total, width), BF16),
            pltpu.VMEM((total, width), BF16),
            dma((3,)),
            dma((experts,)), dma((experts,)), dma((experts,)), dma((experts,)),
            dma((experts,)), dma((experts,)), dma((experts,)), dma((experts,)),
            dma((2 * experts,)), dma((2 * experts,)),
            dma((experts,)), dma((experts,)), dma((experts,)), dma((experts,)),
        ],
        compiler_params=pltpu.CompilerParams(
            collective_id=0, has_side_effects=True, vmem_limit_bytes=60 * 2**20
        ),
    )(
        token_codes,
        jnp.broadcast_to(scales[:, None], (tok, LANES)),
        routes,
        route_gates,
        gate_proj,
        up_proj,
        down_proj,
    )


def solution(mesh):
    placed = (
        P(("groups", "ctx"), None),
        P(("groups", "ctx")),
        P(("groups", "ctx"), None),
        P(("groups", "ctx"), None),
        P("ctx", None, None),
        P("ctx", None, None),
        P("ctx", None, None),
    )
    return jax.shard_map(
        local, mesh=mesh, in_specs=placed, out_specs=P(("groups", "ctx"), None), check_vma=False
    )
```

time: 578 us -> 188 us (0.33)
  the two profiles are of different devices: /device:TPU:15 before, /device:TPU:0 now
where the time goes in v1:
time: 188 us
  Pallas kernels  181 us (96%)
  local copies, waits for them, and re-layouts  6.33 us (3%)
    pallas_call x1, Pallas kernels, local(): pl.pallas_call(functools.partial(kernel, experts, slot, 512), out_shape=j...  181 us
    unnamed x3, local copies, waits for them, and re-layouts  4.98 us

profile of v1, /device:TPU:0, one launch (start us, length us, event | category | flops | bytes accessed | tf_op | source)
XLA Modules:
  0.0 187.7 jit_solution(1649147664905200796)
XLA Ops:
  0.0 1.4 broadcast_in_dim.2.scales
  1.4 1.4 copy.8.routes
  2.8 1.4 copy.9.gates
  4.2 181.3 %shard_map.73 = bf16[128,3584]{1,0:T(8,128)(2,1)} custom-call(s32[128,3584]{1,0:T(8,128)} %codes.1, bf16[128,128]{1,0:T(8,128)(2,1)} %broadcast_in_dim.2.scales, s32[128,2]{1,0:T(8,128)} %copy.8.routes, f32[128,2]{1,0:T(8,128)} %copy.9.gates, bf16[1,3584,384]{2,1,0:T(8,128)(2,1)} %gate_hbm.1, bf16[1,3584,384]{2,1,0:T(8,128)(2,1)} %up_hbm.1, ...), custom_call_target="tpu_custom_call" | custom-call | tf_op jit(solution)/shard_map/pallas_call | solution.py:294
  185.5 2.2 %copy.11 = bf16[128,3584]{1,0:T(8,128)(2,1)} copy(bf16[128,3584]{1,0:T(8,128)(2,1)} %shard_map.73) | data formatting | bytes 1835008

commit v2 on v1

--- a/solution.py
+++ b/solution.py
@@ -9,6 +9,7 @@
 
 SLICES = 4
 LANES = 128
+CHUNKS = 4
 BF16 = jnp.bfloat16
 F32 = jnp.float32
 
@@ -25,14 +26,16 @@
     experts, slot, tile,
     codes, scales, routes, gates, gate_hbm, up_hbm, down_hbm,
     out,
-    w_gu, w_down, pack, recv, gu, hid, part, krecv, ysend, yrecv, hsend, hrecv,
-    w_sem, z_s, z_r, y_s, y_r, c_s, c_r, l_s, l_r, k_s, k_r, q_s, q_r, h_s, h_r,
+    w_gu, w_down, pack, recv, gu, hid, mine, hsend, hrecv,
+    w_sem, z_s, z_r, y_s, y_r, c_s, c_r, l_s, l_r, v_s, v_r, h_s, h_r,
+    wy_s, wy_r, wx_s, wx_r, wl_s, wl_r, wm_s, wm_r, wc_s, wc_r,
 ):
     tok, width = codes.shape
     ff = down_hbm.shape[1]
     quarter = SLICES * slot
     total = experts * slot
     group = lax.axis_index("groups")
+    groups = lax.axis_size("groups")
     me = lax.axis_index("ctx")
     z, row, core = me // 4, (me // 2) % 2, me % 2
 
@@ -54,22 +57,74 @@
     other_core = device(z, row, 1 - core)
     other_row = device(z, 1 - row, core)
 
+    other_both = device(z, 1 - row, 1 - core)
+    block, far_block = row * 2 + core, (1 - row) * 2 + core
+
+    def replica(ahead_by):
+        return ((group + ahead_by) % groups, me)
+
     barrier = pltpu.get_barrier_semaphore()
-    pl.semaphore_signal(barrier, inc=1, device_id=other_core, device_id_type=pl.DeviceIdType.MESH)
-    pl.semaphore_signal(barrier, inc=1, device_id=other_row, device_id_type=pl.DeviceIdType.MESH)
-    for step in range(1, experts):
+    partners = [other_core, other_row, other_both]
+    partners += [device(ahead(step), row, core) for step in range(1, experts)]
+    partners += [replica(by) for by in range(1, groups)]
+    for partner in partners:
         pl.semaphore_signal(
-            barrier, inc=1, device_id=device(ahead(step), row, core),
-            device_id_type=pl.DeviceIdType.MESH,
-        )
+            barrier, inc=1, device_id=partner, device_id_type=pl.DeviceIdType.MESH
+        )
+
+    def block_rows(which):
+        return pl.ds(pl.multiple_of(which * ff, 16), ff)
 
     loads = [
         pltpu.make_async_copy(gate_hbm.at[0], w_gu.at[:, pl.ds(0, ff)], w_sem.at[0]),
         pltpu.make_async_copy(up_hbm.at[0], w_gu.at[:, pl.ds(ff, ff)], w_sem.at[1]),
-        pltpu.make_async_copy(down_hbm.at[0], w_down, w_sem.at[2]),
+        pltpu.make_async_copy(down_hbm.at[0], w_down.at[block_rows(block)], w_sem.at[2]),
     ]
     for load in loads:
         load.start()
+    pl.semaphore_wait(barrier, len(partners))
+
+    share = ff // groups
+    piece = width // CHUNKS
+
+    def share_rows(which, owner):
+        return pl.ds(pl.multiple_of(which * ff + owner * share, 16), share)
+
+    def down_y(q):
+        return remote(
+            down_hbm.at[0, pl.ds(pl.multiple_of(group * share, 16), share), pl.ds(q * piece, piece)],
+            w_down.at[share_rows(block, group), pl.ds(q * piece, piece)],
+            wy_s.at[q], wy_r.at[q], other_row,
+        )
+
+    def down_x(by, q):
+        src = w_down.at[share_rows(far_block, group), pl.ds(q * piece, piece)]
+        at = (by - 1) * CHUNKS + q
+        return remote(src, src, wx_s.at[at], wx_r.at[at], replica(by))
+
+    def down_l(q):
+        src = w_down.at[share_rows(far_block, group), pl.ds(q * piece, piece)]
+        return remote(src, src, wl_s.at[q], wl_r.at[q], other_core)
+
+    def down_m(by):
+        src = w_down.at[share_rows(far_block, (group + groups - by) % groups)]
+        return remote(src, src, wm_s.at[by - 1], wm_r.at[by - 1], other_core)
+
+    down_c = remote(
+        down_hbm.at[0], w_down.at[block_rows(block)], wc_s.at[0], wc_r.at[0], other_core
+    )
+
+    def relay(q):
+        down_y(q).wait_recv()
+        for by in range(1, groups):
+            down_x(by, q).start()
+        down_l(q).start()
+        if q + 2 < CHUNKS:
+            down_y(q + 2).start()
+
+    down_y(0).start()
+    down_y(1).start()
+    down_c.start()
 
     lane = lax.broadcasted_iota(jnp.int32, (tok, LANES), 1)
     named = []
@@ -106,8 +161,6 @@
         recv[pl.ds(own, slot), cols] = rows[:slot]
         pack[:, cols] = rows[slot:]
 
-    pl.semaphore_wait(barrier, experts + 1)
-
     def packet(step, yy, cc):
         return recv.at[pl.ds(pl.multiple_of(step * quarter + (yy * 2 + cc) * slot, 16), slot)]
 
@@ -132,22 +185,20 @@
         src = packet(step, 1 - row, core)
         return remote(src, src, l_s.at[step], l_r.at[step], other_core)
 
-    def part_rows(step, yy, cc):
-        start = (step % 2) * quarter + (yy * 2 + cc) * slot
-        return pl.ds(pl.multiple_of(start, 16), slot)
-
-    def kept(step, yy):
-        return pl.ds(pl.multiple_of((step * 2 + yy) * slot, 16), slot)
-
-    def send_k(step, yy):
+    def hid_rows(step, yy, cc):
+        return pl.ds(pl.multiple_of(step * quarter + (yy * 2 + cc) * slot, 16), slot)
+
+    def step_rows(step):
+        return pl.ds(pl.multiple_of(step * slot, 16), slot)
+
+    own_cols = pl.ds(pl.multiple_of(block * ff, LANES), ff)
+
+    def send_v(step, number):
+        yy = 1 - row if number > 0 else row
+        cc = 1 - core if number != 1 else core
         return remote(
-            part.at[part_rows(step, yy, 1 - core)], krecv.at[kept(step, yy)],
-            k_s.at[step * 2 + yy], k_r.at[step * 2 + yy], other_core,
-        )
-
-    def send_q(step):
-        return remote(
-            slab(ysend, step % 2), slab(yrecv, step), q_s.at[step], q_r.at[step], other_row
+            hid.at[hid_rows(step, yy, cc)], mine.at[step_rows(step), own_cols],
+            v_s.at[step * 3 + number], v_r.at[step * 3 + number], device(z, yy, cc),
         )
 
     def send_h(step):
@@ -156,53 +207,15 @@
             device(behind(step), row, core),
         )
 
-    for step in range(1, experts):
-        send_z(step).start()
-    send_y(0).start()
-    send_c(0).start()
-    for load in loads:
-        load.wait()
-
-    def finish(step):
-        send_k(step, row).wait_recv()
-        send_q(step).wait_recv()
-
-        @pl.loop(0, width // tile)
-        def _(n):
-            cols = pl.ds(pl.multiple_of(n * tile, tile), tile)
-            value = (
-                part[part_rows(step, row, core), cols].astype(F32)
-                + krecv[kept(step, row), cols].astype(F32)
-                + slab(yrecv, step)[:, cols].astype(F32)
-            ).astype(BF16)
-
-            @pl.when(step > 0)
-            def _():
-                hsend[pl.ds(pl.multiple_of(step * slot, 16), slot), cols] = value
-
-            @pl.when(step == 0)
-            def _():
-                hrecv[pl.ds(0, slot), cols] = value
-
-        @pl.when(step > 0)
-        def _():
-            send_h(step).start()
-
-        send_k(step, 0).wait_send()
-        send_k(step, 1).wait_send()
-
-    def one_group(step, carry):
-        @pl.when(step + 1 < experts)
-        def _():
-            send_z(step + 1).wait_recv()
-            send_y(step + 1).start()
-            send_c(step + 1).start()
-
+    def spread(step):
+        send_y(step).start()
+        send_c(step).start()
+
+    def hidden(step):
         send_y(step).wait_recv()
         send_l(step).start()
         send_c(step).wait_recv()
         send_l(step).wait_recv()
-
         rows = pl.ds(pl.multiple_of(step * quarter, 16), quarter)
 
         @pl.loop(0, 2 * ff // 256)
@@ -219,44 +232,74 @@
             scale = recv[where, pl.ds(width, LANES)].astype(F32)[:, :1]
             a = gu[some, pl.ds(0, ff)] * scale
             b = gu[some, pl.ds(ff, ff)] * scale
-            hid[some, :] = (a / (1.0 + jnp.exp(-a)) * b).astype(BF16)
-
-        base = pl.ds(pl.multiple_of((step % 2) * quarter, 16), quarter)
+            hid[where, :] = (a / (1.0 + jnp.exp(-a)) * b).astype(BF16)
+
+        for number in range(3):
+            send_v(step, number).start()
+        mine[step_rows(step), own_cols] = hid[hid_rows(step, row, core), :]
+
+    def project(step, target):
+        for number in range(3):
+            send_v(step, number).wait_recv()
 
         @pl.loop(0, width // tile)
         def _(n):
             cols = pl.ds(pl.multiple_of(n * tile, tile), tile)
-            part[base, cols] = jnp.dot(
-                hid[...], w_down[:, cols], preferred_element_type=F32
+            target[step_rows(step), cols] = jnp.dot(
+                mine[step_rows(step), :], w_down[:, cols], preferred_element_type=F32
             ).astype(BF16)
 
-        send_k(step, 1 - row).start()
-        send_k(step, row).start()
-
-        @pl.when(step >= 2)
-        def _():
-            send_q(step - 2).wait_send()
-
-        send_k(step, 1 - row).wait_recv()
-
-        @pl.loop(0, width // tile)
-        def _(n):
-            cols = pl.ds(pl.multiple_of(n * tile, tile), tile)
-            ysend[pl.ds(pl.multiple_of((step % 2) * slot, 16), slot), cols] = (
-                part[part_rows(step, 1 - row, core), cols].astype(F32)
-                + krecv[kept(step, 1 - row), cols].astype(F32)
-            ).astype(BF16)
-
-        send_q(step).start()
-
-        @pl.when(step > 0)
-        def _():
-            finish(step - 1)
+    send_z(1).start()
+    relay(0)
+    relay(1)
+    send_z(1).wait_recv()
+    spread(1)
+    if experts > 2:
+        send_z(2).start()
+    for q in range(2, CHUNKS):
+        relay(q)
+    for load in loads:
+        load.wait()
+    hidden(1)
+    for by in range(1, groups):
+        for q in range(CHUNKS):
+            down_x(by, q).wait_recv()
+        down_m(by).start()
+
+    def one_group(step, carry):
+        @pl.when(step + 1 < experts)
+        def _():
+            send_z(step + 1).wait_recv()
+            spread(step + 1)
+
+        @pl.when(step + 2 < experts)
+        def _():
+            send_z(step + 2).start()
+
+        @pl.when(step == 1)
+        def _():
+            down_c.wait_recv()
+            for q in range(CHUNKS):
+                down_l(q).wait_recv()
+            for by in range(1, groups):
+                down_m(by).wait_recv()
+
+        project(step, hsend)
+        send_h(step).start()
+
+        @pl.when(step == experts - 2)
+        def _():
+            spread(0)
+
+        @pl.when(step + 1 < experts)
+        def _():
+            hidden(step + 1)
 
         return carry
 
-    lax.fori_loop(0, experts, one_group, 0)
-    finish(experts - 1)
+    lax.fori_loop(1, experts, one_group, 0)
+    hidden(0)
+    project(0, hrecv)
 
     for step in range(1, experts):
         send_h(step).wait_recv()
@@ -270,12 +313,20 @@
             + jnp.dot(mix_lo, rows, preferred_element_type=F32)
         ).astype(BF16)
 
+    for q in range(CHUNKS):
+        down_y(q).wait_send()
+        down_l(q).wait_send()
+        for by in range(1, groups):
+            down_x(by, q).wait_send()
+    for by in range(1, groups):
+        down_m(by).wait_send()
+    down_c.wait_send()
     for step in range(experts):
         send_y(step).wait_send()
         send_c(step).wait_send()
         send_l(step).wait_send()
-        if step >= experts - 2:
-            send_q(step).wait_send()
+        for number in range(3):
+            send_v(step, number).wait_send()
         if step > 0:
             send_z(step).wait_send()
             send_h(step).wait_send()
@@ -291,6 +342,8 @@
     vmem = pl.BlockSpec(memory_space=pltpu.VMEM)
     hbm = pl.BlockSpec(memory_space=pl.ANY)
     dma = pltpu.SemaphoreType.DMA
+    groups = lax.axis_size("groups")
+    far = max(1, (groups - 1) * CHUNKS)
     return pl.pallas_call(
         functools.partial(kernel, experts, slot, 512),
         out_shape=jax.ShapeDtypeStruct((tok, width), BF16),
@@ -298,22 +351,22 @@
         out_specs=vmem,
         scratch_shapes=[
             pltpu.VMEM((width, 2 * ff), BF16),
-            pltpu.VMEM((ff, width), BF16),
+            pltpu.VMEM((SLICES * ff, width), BF16),
             pltpu.VMEM((total - slot, width + LANES), BF16),
             pltpu.VMEM((SLICES * total, width + LANES), BF16),
             pltpu.VMEM((SLICES * slot, 2 * ff), F32),
-            pltpu.VMEM((SLICES * slot, ff), BF16),
-            pltpu.VMEM((2 * SLICES * slot, width), BF16),
-            pltpu.VMEM((2 * total, width), BF16),
-            pltpu.VMEM((2 * slot, width), BF16),
-            pltpu.VMEM((total, width), BF16),
+            pltpu.VMEM((SLICES * total, ff), BF16),
+            pltpu.VMEM((total, SLICES * ff), BF16),
             pltpu.VMEM((total, width), BF16),
             pltpu.VMEM((total, width), BF16),
             dma((3,)),
             dma((experts,)), dma((experts,)), dma((experts,)), dma((experts,)),
             dma((experts,)), dma((experts,)), dma((experts,)), dma((experts,)),
-            dma((2 * experts,)), dma((2 * experts,)),
-            dma((experts,)), dma((experts,)), dma((experts,)), dma((experts,)),
+            dma((3 * experts,)), dma((3 * experts,)),
+            dma((experts,)), dma((experts,)),
+            dma((CHUNKS,)), dma((CHUNKS,)), dma((far,)), dma((far,)),
+            dma((CHUNKS,)), dma((CHUNKS,)), dma((groups,)), dma((groups,)),
+            dma((1,)), dma((1,)),
         ],
         compiler_params=pltpu.CompilerParams(
             collective_id=0, has_side_effects=True, vmem_limit_bytes=60 * 2**20

time: 188 us -> 152 us (0.81)
  Pallas kernels: 181 us -> 145 us
    pallas_call x1, Pallas kernels: 181 us -> 145 us  [local(): pl.pallas_call(functools.partial(kernel, experts, slot, 512), out_shape=j...]
where the time goes in v2:
time: 152 us; the launch traced here: 151 us
  Pallas kernels  145 us (95%)
  local copies, waits for them, and re-layouts  6.33 us (4%)
    pallas_call x1, Pallas kernels, local(): pl.pallas_call(functools.partial(kernel, experts, slot, 512), out_shape=j...  145 us
    unnamed x3, local copies, waits for them, and re-layouts  4.98 us

profile of v2, /device:TPU:0, one launch (start us, length us, event | category | flops | bytes accessed | tf_op | source)
XLA Modules:
  0.0 151.3 jit_solution(11672662987299520661)
XLA Ops:
  0.0 1.4 broadcast_in_dim.2.scales
  1.4 1.4 copy.8.routes
  2.8 1.4 copy.9.gates
  4.2 145.0 %shard_map.73 = bf16[128,3584]{1,0:T(8,128)(2,1)} custom-call(s32[128,3584]{1,0:T(8,128)} %codes.1, bf16[128,128]{1,0:T(8,128)(2,1)} %broadcast_in_dim.2.scales, s32[128,2]{1,0:T(8,128)} %copy.8.routes, f32[128,2]{1,0:T(8,128)} %copy.9.gates, bf16[1,3584,384]{2,1,0:T(8,128)(2,1)} %gate_hbm.1, bf16[1,3584,384]{2,1,0:T(8,128)(2,1)} %up_hbm.1, ...), custom_call_target="tpu_custom_call" | custom-call | tf_op jit(solution)/shard_map/pallas_call | solution.py:347
  149.2 2.2 %copy.11 = bf16[128,3584]{1,0:T(8,128)(2,1)} copy(bf16[128,3584]{1,0:T(8,128)(2,1)} %shard_map.73) | data formatting | bytes 1835008

commit v3 on v2

--- a/solution.py
+++ b/solution.py
@@ -201,9 +201,14 @@
             v_s.at[step * 3 + number], v_r.at[step * 3 + number], device(z, yy, cc),
         )
 
-    def send_h(step):
+    tiles = width // tile
+    cuts = (0, (tiles + 1) // 2, tiles)
+
+    def send_h(step, half):
+        cols = pl.ds(cuts[half] * tile, (cuts[half + 1] - cuts[half]) * tile)
         return remote(
-            slab(hsend, step), slab(hrecv, step), h_s.at[step], h_r.at[step],
+            hsend.at[step_rows(step), cols], hrecv.at[step_rows(step), cols],
+            h_s.at[step * 2 + half], h_r.at[step * 2 + half],
             device(behind(step), row, core),
         )
 
@@ -238,11 +243,8 @@
             send_v(step, number).start()
         mine[step_rows(step), own_cols] = hid[hid_rows(step, row, core), :]
 
-    def project(step, target):
-        for number in range(3):
-            send_v(step, number).wait_recv()
-
-        @pl.loop(0, width // tile)
+    def project(step, target, half):
+        @pl.loop(cuts[half], cuts[half + 1])
         def _(n):
             cols = pl.ds(pl.multiple_of(n * tile, tile), tile)
             target[step_rows(step), cols] = jnp.dot(
@@ -284,8 +286,11 @@
             for by in range(1, groups):
                 down_m(by).wait_recv()
 
-        project(step, hsend)
-        send_h(step).start()
+        for number in range(3):
+            send_v(step, number).wait_recv()
+        for half in range(2):
+            project(step, hsend, half)
+            send_h(step, half).start()
 
         @pl.when(step == experts - 2)
         def _():
@@ -299,10 +304,14 @@
 
     lax.fori_loop(1, experts, one_group, 0)
     hidden(0)
-    project(0, hrecv)
+    for number in range(3):
+        send_v(0, number).wait_recv()
+    for half in range(2):
+        project(0, hrecv, half)
 
     for step in range(1, experts):
-        send_h(step).wait_recv()
+        for half in range(2):
+            send_h(step, half).wait_recv()
 
     @pl.loop(0, width // tile)
     def _(n):
@@ -329,7 +338,8 @@
             send_v(step, number).wait_send()
         if step > 0:
             send_z(step).wait_send()
-            send_h(step).wait_send()
+            for half in range(2):
+                send_h(step, half).wait_send()
 
 
 def local(token_codes, scales, routes, route_gates, gate_proj, up_proj, down_proj):
@@ -363,7 +373,7 @@
             dma((experts,)), dma((experts,)), dma((experts,)), dma((experts,)),
             dma((experts,)), dma((experts,)), dma((experts,)), dma((experts,)),
             dma((3 * experts,)), dma((3 * experts,)),
-            dma((experts,)), dma((experts,)),
+            dma((2 * experts,)), dma((2 * experts,)),
             dma((CHUNKS,)), dma((CHUNKS,)), dma((far,)), dma((far,)),
             dma((CHUNKS,)), dma((CHUNKS,)), dma((groups,)), dma((groups,)),
             dma((1,)), dma((1,)),

time: 152 us -> 151 us (level)
  no operation moved by 1% of the time
where the time goes in v3:
time: 151 us; the launch traced here: 150 us
  Pallas kernels  144 us (95%)
  local copies, waits for them, and re-layouts  6.33 us (4%)
    pallas_call x1, Pallas kernels, local(): pl.pallas_call(functools.partial(kernel, experts, slot, 512), out_shape=j...  144 us
    unnamed x3, local copies, waits for them, and re-layouts  4.98 us

profile of v3, /device:TPU:0, one launch (start us, length us, event | category | flops | bytes accessed | tf_op | source)
XLA Modules:
  0.0 150.4 jit_solution(14581391339893359488)
XLA Ops:
  0.0 1.4 broadcast_in_dim.2.scales
  1.4 1.4 copy.8.routes
  2.8 1.4 copy.9.gates
  4.2 144.0 %shard_map.73 = bf16[128,3584]{1,0:T(8,128)(2,1)} custom-call(s32[128,3584]{1,0:T(8,128)} %codes.1, bf16[128,128]{1,0:T(8,128)(2,1)} %broadcast_in_dim.2.scales, s32[128,2]{1,0:T(8,128)} %copy.8.routes, f32[128,2]{1,0:T(8,128)} %copy.9.gates, bf16[1,3584,384]{2,1,0:T(8,128)(2,1)} %gate_hbm.1, bf16[1,3584,384]{2,1,0:T(8,128)(2,1)} %up_hbm.1, ...), custom_call_target="tpu_custom_call" | custom-call | tf_op jit(solution)/shard_map/pallas_call | solution.py:357
  148.2 2.2 %copy.11 = bf16[128,3584]{1,0:T(8,128)(2,1)} copy(bf16[128,3584]{1,0:T(8,128)(2,1)} %shard_map.73) | data formatting | bytes 1835008
